TPU v7x, 32 devices: a whole 2x2x4 slice. The times are simulated.
32 devices in a mesh: row: 4 (over z), depth: 8 (over y, x, core).
Axes of the slice: x: 2, y: 2, z: 4, core: 2. Of those that a mesh axis runs over, the one named last changes fastest.
Arguments:
- table: float32 [4, 1024, 256], P(None, 'row'), may hold values from -6 to 6
- accum: float32 [4, 1024], P(None, 'row'), may hold values from 0.0001 to 0.01
- owner: int32 [256, 4, 64, 1], P(('row', 'depth')), may hold values from 0 to 3; in each aligned block of 2048 rows (0 to 2047, 2048 to 4095, ..., all dimensions but the last counted through in order) at most 1024 rows name the same one
- local_row: int32 [256, 4, 64], P(('row', 'depth')), may hold values from 0 to 255
- lengths: int32 [256, 4], P(('row', 'depth')), may hold values from 1 to 64
- dense_q: int32 [256, 13], P(('row', 'depth')), may hold values from 0 to 255
- labels: int32 [256], P(('row', 'depth')), may hold values 0 or 1
- bottom_w: float32 [13, 256], replicated, may hold values from -1.75 to 1.75
- top_w: float32 [10], replicated, may hold values from -4 to 4
Outputs:
- new_table: float32 [4, 1024, 256], P(None, 'row')
- new_accum: float32 [4, 1024], P(None, 'row')
- logits: float32 [256], P(('row', 'depth'))
Inputs may be any that keep to these rules, and one draw needn't show every extreme that they name: `owner`: among the id slots of one device (aligned blocks of 2048 slots, padding slots included), no value is named more than 1024 times, a bound that some block reaches.
All inputs are finite; a program needn't handle non-finite values. No bound on the sum of `labels` on one device may be relied on, other than what follows from the above.
Results may differ from a plain program's by a relative error of at most 0.00012.
Values sent between devices are 32-bit elements; how exact they have to be, the bound alone decides.
A program may use at most 64 MiB of HBM per device.

v0:
```python
import jax
import jax.numpy as jnp
import numpy as np
from jax import lax
from jax.sharding import PartitionSpec as P

LEARN_RATE = 0.5
EPSILON = 1e-08


def pair_matrix(top_w, count):
    upper_i, upper_k = np.triu_indices(count, 1)
    matrix = jnp.zeros((count, count), jnp.float32)
    matrix = matrix.at[upper_i, upper_k].set(top_w)
    return matrix.at[upper_k, upper_i].set(top_w)


def adagrad(rows_now, state_now, gradient):
    state = state_now + jnp.mean(gradient * gradient, axis=1)
    return (rows_now - LEARN_RATE * gradient / (jnp.sqrt(state)[:, None] + EPSILON), state)


def shards(table, accum, owner, local_row, lengths, dense_q, labels, bottom_w, top_w):
    tables, rows_dev, features = table.shape
    samples, bag_size = (owner.shape[0], owner.shape[2])
    row_devices = lax.axis_size("row")
    slot_count = samples * tables * bag_size
    bag_count = samples * tables
    capacity = 2 * slot_count // row_devices
    row_span = tables * rows_dev
    owner_of = owner.reshape(slot_count)
    local_of = local_row.reshape(slot_count)
    slot_live = (
        lax.broadcasted_iota(jnp.int32, (samples, tables, bag_size), 2) < lengths[:, :, None]
    ).reshape(slot_count)
    slot_index = jnp.arange(slot_count, dtype=jnp.int32)
    bag_of = slot_index // bag_size
    table_of = bag_of % tables
    entry_codes = jnp.where(slot_live, bag_of * row_span + table_of * rows_dev + local_of, -1)
    owner_hits = (owner_of[:, None] == jnp.arange(row_devices, dtype=jnp.int32)[None, :]).astype(
        jnp.int32
    )
    before = jnp.cumsum(owner_hits, axis=0) - owner_hits
    position = jnp.sum(before * owner_hits, axis=1)
    outgoing = (
        jnp.full((row_devices * capacity,), -1, jnp.int32)
        .at[owner_of * capacity + position]
        .set(entry_codes)
    )
    received = lax.all_to_all(
        outgoing.reshape(row_devices, capacity), "row", split_axis=0, concat_axis=0, tiled=True
    )
    is_live = received >= 0
    flat_rows = jnp.where(is_live, received % row_span, 0)
    bag_at = jnp.where(is_live, received // row_span, -1)
    flat_table = table.reshape(row_span, features)
    picked = flat_table[flat_rows]
    choose = (bag_at[:, None, :] == jnp.arange(bag_count, dtype=jnp.int32)[None, :, None]).astype(
        jnp.float32
    )
    partial_pool = jnp.einsum("sbc,scw->sbw", choose, picked, precision=lax.Precision.HIGHEST)
    returned = lax.all_to_all(partial_pool, "row", split_axis=0, concat_axis=0, tiled=True)
    pooled = jnp.sum(returned, axis=0).reshape(samples, tables, features)
    dequant = (dense_q.astype(jnp.float32) - 128.0) / 64.0
    dense_vec = jnp.dot(dequant, bottom_w, precision=lax.Precision.HIGHEST)
    bag_scale = float(bag_size) ** (-0.5)
    width_scale = float(features) ** (-0.5)
    vectors = jnp.concatenate([dense_vec[:, None, :], bag_scale * pooled], axis=1)
    dots = width_scale * jnp.einsum(
        "biw,bkw->bik", vectors, vectors, precision=lax.Precision.HIGHEST
    )
    matrix = pair_matrix(top_w, tables + 1)
    logits = 0.5 * jnp.sum(dots * matrix[None, :, :], axis=(1, 2))
    loss_coeff = (jax.nn.sigmoid(logits) - labels.astype(jnp.float32)) * bag_scale * width_scale
    mixed = jnp.einsum("ti,biw->btw", matrix[1:, :], vectors, precision=lax.Precision.HIGHEST)
    pooled_grad = (loss_coeff[:, None, None] * mixed).reshape(1, bag_count, features)
    piece = lax.all_gather(pooled_grad, "row", axis=0, tiled=True)
    piece_sources = piece.shape[0]
    piece_live = received >= 0
    piece_bags = jnp.where(piece_live, received // row_span, 0)
    source_at = jnp.arange(piece_sources, dtype=jnp.int32)[:, None]
    slot_grads = piece[source_at, piece_bags] * piece_live[:, :, None].astype(jnp.float32)
    row_grad = (
        jnp.zeros((row_span, features), jnp.float32)
        .at[flat_rows.reshape(-1)]
        .add(slot_grads.reshape(-1, features))
    )
    flat_accum = accum.reshape(row_span)
    summed = lax.psum(row_grad, "depth")
    new_rows, new_state = adagrad(flat_table, flat_accum, summed)
    return (
        new_rows.reshape(tables, rows_dev, features),
        new_state.reshape(tables, rows_dev),
        logits,
    )


def solution(mesh):
    in_specs = (
        P(None, "row", None),
        P(None, "row"),
        P(("row", "depth"), None, None, None),
        P(("row", "depth"), None, None),
        P(("row", "depth"), None),
        P(("row", "depth"), None),
        P(("row", "depth")),
        P(),
        P(),
    )
    out_specs = (P(None, "row", None), P(None, "row"), P(("row", "depth")))
    return jax.shard_map(shards, mesh=mesh, in_specs=in_specs, out_specs=out_specs, check_vma=False)
```

profile of v0, /device:TPU:1, one launch (start us, length us, event | category | flops | bytes accessed | tf_op | source)
XLA Modules:
  0.0 199.9 jit_solution(15882114160335495467)
XLA Ops:
  7.2 0.0 copy-start
  7.2 0.0 copy-start.1
  7.2 0.9 eq.48
  8.1 1.1 reduce-window.6
  9.2 0.2 slice_reduce_fusion
  9.4 0.2 reduce-window.9
  9.6 0.1 add_bitcast_fusion
  9.7 0.5 broadcast.440
  10.2 1.5 fusion.37
  11.7 0.1 eq.44
  11.8 0.1 mul.87
  11.9 0.8 copy.22
  12.6 0.1 iota_compare_fusion.4
  12.7 0.1 lt.77
  12.8 0.8 reshape.326
  13.7 8.6 %scatter_custom_fusion = s32[4096]{0:T(1024)} fusion(s32[2048]{0:T(1024)S(1)} %bitcast.80, s32[2048]{0:T(1024)S(1)} %fusion.17, s32[]{:T(128)} %constant.96.clone.1), kind=kCustom, calls=%fused_computation.74 | custom fusion | bytes 16388 | tf_op jit(solution)/shard_map/scatter | solution.py:48
  22.3 5.4 %all-to-all-start = ((s32[4,1,1024]{2,1,0:T(1,128)}), s32[4,1,1024]{2,1,0:T(1,128)S(1)}, u32[]{:S(2)}, u32[]{:S(2)}) async-start(s32[4,1,1024]{2,1,0:T(1,128)} %bitcast.4), calls=%async_computation | async-start | bytes 32768 | tf_op jit(solution)/shard_map/all_to_all | solution.py:50
  27.7 1.7 scatter_fusion
  29.5 1.7 scatter_fusion.1
  31.2 0.0 copy-done
  31.2 0.8 convolution_bitcast_fusion
  32.1 0.1 all-to-all-done
  32.2 0.2 shift-left_or_fusion
  32.4 0.1 compare_select_fusion.15
  32.5 0.0 copy-done.1
  32.5 16.1 %gather_fusion = f32[4096,256]{1,0:T(8,128)} fusion(f32[1024,256]{1,0:T(8,128)S(1)} %bitcast.67, s32[4096]{0:T(1024)S(1)} %broadcast_clamp_fusion), kind=kCustom, calls=%fused_computation | custom fusion | bytes 8404992 | tf_op jit(solution)/shard_map/gather | solution.py:57
  48.6 0.0 copy-start.3
  48.6 0.0 copy-start.2
  48.6 4.5 %fusion.6 = f32[4,32,256]{2,1,0:T(8,128)} fusion(f32[4,1024,256]{2,1,0:T(8,128)} %bitcast.68, s32[4,1024]{1,0:T(4,128)S(1)} %bitcast.73), kind=kOutput, calls=%fused_computation.18 | convolution fusion | flops 402784256 | bytes 4341760 | tf_op jit(solution)/shard_map/sbc,scw->sbw/dot_general | solution.py:61
  53.1 4.4 %all-to-all-start.1 = ((f32[4,32,256]{2,1,0:T(8,128)}), f32[4,32,256]{2,1,0:T(8,128)S(1)}, u32[]{:S(2)}, u32[]{:S(2)}) async-start(f32[4,32,256]{2,1,0:T(8,128)} %fusion.6), calls=%async_computation.1 | async-start | bytes 262144 | tf_op jit(solution)/shard_map/all_to_all | solution.py:62
  57.5 0.0 all-reduce.2.cloned.1.call-start
  57.5 0.1 compare_select_fusion.2
  57.6 4.7 %all-to-all-done.1 = f32[4,32,256]{2,1,0:T(8,128)S(1)} async-done(((f32[4,32,256]{2,1,0:T(8,128)}), f32[4,32,256]{2,1,0:T(8,128)S(1)}, u32[]{:S(2)}, u32[]{:S(2)}) %all-to-all-start.1) | async-done | bytes 131104 | tf_op jit(solution)/shard_map/all_to_all | solution.py:62
  62.4 0.3 fusion.4
  62.7 0.0 copy-done.3
  62.7 0.5 fusion.31
  63.2 0.2 fusion.3
  63.4 11.1 %all_gather.3 = f32[4,32,256]{2,1,0:T(8,128)S(1)} all-gather(f32[1,32,256]{2,1,0:T(8,128)S(1)} %reshape.327), channel_id=1, replica_groups=mesh['row'=4,'depth'=8] {'row'}, dimensions={0}, use_global_device_ids=true | all-gather | bytes 163840 | tf_op jit(solution)/shard_map/all_gather | solution.py:77
  74.5 53.2 %scatter_custom_fusion.3 = f32[1024,256]{1,0:T(8,128)} fusion(s32[4096]{0:T(1024)S(1)} %bitcast.78, f32[4096]{0:T(1024)S(1)} %bitcast.72, f32[]{:T(128)} %constant.95.clone.1, f32[4,32,256]{2,1,0:T(8,128)S(1)} %all_gather.3, s32[4096]{0:T(1024)S(1)} %bitcast.71), kind=kCustom, calls=%fused_computation.6 | custom fusion | flops 2097152 | bytes 1212420 | tf_op jit(solution)/shard_map/scatter-add | solution.py:86
  127.7 0.0 all-reduce.2.cloned.1.call-update
  127.7 0.0 copy-done.2
  127.7 60.9 %all-reduce.2.cloned.1.call-done = f32[1024,256]{1,0:T(8,128)} async-done(((f32[1024,256]{1,0:T(8,128)}), f32[1024,256]{1,0:T(8,128)}) %all-reduce.2.cloned.1.call-update) | async-done | bytes 1048592 | tf_op jit(solution)/shard_map/psum | solution.py:89
  188.6 1.4 multiply_reduce_fusion
  190.1 0.6 add.159
  190.7 2.4 %divide_subtract_fusion = f32[1024,256]{1,0:T(8,128)} fusion(f32[1024,256]{1,0:T(8,128)} %all-reduce.2.cloned.1.call-done, f32[1024]{0:T(1024)S(1)} %get-tuple-element.10, f32[4,256,256]{2,1,0:T(8,128)S(1)} %copy-done.1), kind=kLoop, calls=%fused_computation.14 | loop fusion | flops 786432 | bytes 3149824 | tf_op jit(solution)/shard_map/sub | solution.py:20
  (17 shorter events, 0.2 us)
Async XLA Ops:
  7.2 24.1 %copy-start = (f32[13,256]{1,0:T(8,128)S(1)}, f32[13,256]{1,0:T(8,128)}, u32[]{:S(2)}) copy-start(f32[13,256]{1,0:T(8,128)} %param.22) | copy-start | bytes 39940
  7.2 25.3 %copy-start.1 = (f32[4,256,256]{2,1,0:T(8,128)S(1)}, f32[4,256,256]{2,1,0:T(8,128)}, u32[]{:S(2)}) copy-start(f32[4,256,256]{2,1,0:T(8,128)} %param.15) | copy-start | bytes 3145732
  22.3 9.9 %all-to-all-start = ((s32[4,1,1024]{2,1,0:T(1,128)}), s32[4,1,1024]{2,1,0:T(1,128)S(1)}, u32[]{:S(2)}, u32[]{:S(2)}) async-start(s32[4,1,1024]{2,1,0:T(1,128)} %bitcast.4), calls=%async_computation | async-start | bytes 32768 | tf_op jit(solution)/shard_map/all_to_all | solution.py:50
  48.6 14.1 %copy-start.3 = (s32[8]{0:T(128)S(1)}, s32[8]{0:T(128)}, u32[]{:S(2)}) copy-start(s32[8]{0:T(128)} %param.21) | copy-start | bytes 100
  48.6 79.2 %copy-start.2 = (f32[4,256]{1,0:T(4,128)S(1)}, f32[4,256]{1,0:T(4,128)}, u32[]{:S(2)}) copy-start(f32[4,256]{1,0:T(4,128)} %param.16) | copy-start | bytes 12292
  53.1 9.2 %all-to-all-start.1 = ((f32[4,32,256]{2,1,0:T(8,128)}), f32[4,32,256]{2,1,0:T(8,128)S(1)}, u32[]{:S(2)}, u32[]{:S(2)}) async-start(f32[4,32,256]{2,1,0:T(8,128)} %fusion.6), calls=%async_computation.1 | async-start | bytes 262144 | tf_op jit(solution)/shard_map/all_to_all | solution.py:62
  57.5 131.1 %all-reduce.2.cloned.1.call-start = ((), (), s32[]{:S(2)}) async-start(), calls=%async_computation.2 | async-start | bytes 2097152 | tf_op jit(solution)/shard_map/psum | solution.py:89
Sparse Core Ops, SparseCore 0:
  127.8 60.7 all-reduce.1
where the time goes:
time: 202 us; the launch traced here: 200 us
  waiting for transfers between devices  65.7 us (33%)
  other arithmetic  61.6 us (30%)
  local copies, waits for them, and re-layouts  31.7 us (16%)
  between operations  14.2 us (7%)
  blocking collectives  11.1 us (5%)
  starting transfers between devices  9.87 us (5%)
  matrix products  5.84 us (3%)
    psum x1, waiting for transfers between devices, shards(): summed = lax.psum(row_grad, 'depth')  60.9 us
    scatter-add x1, other arithmetic, shards(): row_grad = jnp.zeros((row_span, features), jnp.float32).at[flat_rows.resh...  53.2 us
    gather x1, local copies, waits for them, and re-layouts, shards(): picked = flat_table[flat_rows]  16.1 us
    all_gather x1, blocking collectives, shards(): piece = lax.all_gather(pooled_grad, 'row', axis=0, tiled=True)  11.1 us
    scatter x1, local copies, waits for them, and re-layouts, shards(): outgoing = jnp.full((row_devices * capacity,), -1, jnp.int32).at[owner_of...  8.62 us
    all_to_all x1, starting transfers between devices, shards(): lax.all_to_all(outgoing.reshape(row_devices, capacity), 'row', split_axis...  5.42 us
    all_to_all x1, waiting for transfers between devices, shards(): lax.all_to_all(partial_pool, 'row', split_axis=0, concat_axis=0, tiled=True)  4.68 us
    dot_general x1, matrix products, shards(): jnp.einsum('sbc,scw->sbw', choose, picked, precision=lax.Precision.HIGHEST)  4.51 us
  transfers between devices with their start and end apart: 3, of which 3 were waited for; matrix products, arithmetic and copies ran while one was open for 2% of the time, Pallas kernels for 0%

commit v1 on v0

--- a/solution.py
+++ b/solution.py
@@ -1,7 +1,11 @@
+import functools
+
 import jax
 import jax.numpy as jnp
 import numpy as np
 from jax import lax
+from jax.experimental import pallas as pl
+from jax.experimental.pallas import tpu as pltpu
 from jax.sharding import PartitionSpec as P
 
 LEARN_RATE = 0.5
@@ -20,7 +24,7 @@
     return (rows_now - LEARN_RATE * gradient / (jnp.sqrt(state)[:, None] + EPSILON), state)
 
 
-def shards(table, accum, owner, local_row, lengths, dense_q, labels, bottom_w, top_w):
+def shards_large(table, accum, owner, local_row, lengths, dense_q, labels, bottom_w, top_w):
     tables, rows_dev, features = table.shape
     samples, bag_size = (owner.shape[0], owner.shape[2])
     row_devices = lax.axis_size("row")
@@ -95,6 +99,358 @@
     )
 
 
+def remote(src, dst, send_sem, recv_sem, device):
+    return pltpu.make_async_remote_copy(
+        src_ref=src,
+        dst_ref=dst,
+        send_sem=send_sem,
+        recv_sem=recv_sem,
+        device_id=device,
+        device_id_type=pl.DeviceIdType.MESH,
+    )
+
+
+def two_terms(value):
+    high = value.astype(jnp.bfloat16)
+    return high, (value - high.astype(jnp.float32)).astype(jnp.bfloat16)
+
+
+def matmul(a, b):
+    return lax.dot_general(a, b, (((1,), (0,)), ((), ())), preferred_element_type=jnp.float32)
+
+
+def step_kernel(
+    table,
+    accum,
+    owner,
+    local_row,
+    lengths,
+    dense_q,
+    labels,
+    bottom_w,
+    top_w,
+    new_table,
+    new_accum,
+    logits_out,
+    codes,
+    counts,
+    partials,
+    pools,
+    grads,
+    weights,
+    state_cols,
+    code_send,
+    code_recv,
+    count_send,
+    count_pass,
+    count_recv,
+    pool_send,
+    pool_recv,
+    grad_send,
+    grad_spread,
+    grad_pass,
+    grad_recv,
+):
+    rows = codes.shape[0]
+    depths = counts.shape[0]
+    half = depths // 2
+    tables, rows_dev, features = table.shape
+    samples, _, bag_size = owner.shape
+    r = lax.axis_index("row")
+    d = lax.axis_index("depth")
+    partner = d + 1 - 2 * lax.rem(d, 2)
+    row_peers = [lax.rem(r + k, rows) for k in range(1, rows)]
+    depth_peers = [lax.rem(d + 2 * k, depths) for k in range(1, half)]
+    partner_side = [partner] + [lax.rem(partner + 2 * k, depths) for k in range(1, half)]
+
+    barrier = pltpu.get_barrier_semaphore()
+    for peer in row_peers:
+        pl.semaphore_signal(
+            barrier, inc=1, device_id={"row": peer}, device_id_type=pl.DeviceIdType.MESH
+        )
+    for peer in depth_peers + [partner]:
+        pl.semaphore_signal(
+            barrier, inc=1, device_id={"depth": peer}, device_id_type=pl.DeviceIdType.MESH
+        )
+
+    slot_at = lax.broadcasted_iota(jnp.int32, (samples, bag_size), 1)
+    mine = []
+    for t in range(tables):
+        live = slot_at < lengths[:, t : t + 1]
+        mine.append(jnp.where(live, owner[:, t, :] * rows_dev + local_row[:, t, :], -1))
+    for p in range(tables // 2):
+        codes[r, p] = jnp.concatenate([mine[2 * p], mine[2 * p + 1]], axis=1)
+
+    pl.semaphore_wait(barrier, rows - 1 + half)
+
+    code_copies = [
+        remote(codes.at[r], codes.at[r], code_send.at[i], code_recv.at[r], {"row": peer})
+        for i, peer in enumerate(row_peers)
+    ]
+    for copy in code_copies:
+        copy.start()
+
+    row_at = lax.broadcasted_iota(jnp.int32, (samples, rows_dev), 1)
+
+    def count(source):
+        def pair(p, carry):
+            relative = codes[source, p] - r * rows_dev
+            for side in range(2):
+                total = jnp.zeros((samples, rows_dev), jnp.float32)
+                for j in range(bag_size):
+                    at = side * bag_size + j
+                    total = total + jnp.where(relative[:, at : at + 1] == row_at, 1.0, 0.0)
+                counts[d, source, 2 * p + side] = total
+            return carry
+
+        lax.fori_loop(0, tables // 2, pair, 0)
+
+    count(r)
+
+    def count_peer(k, carry):
+        source = lax.rem(r + k, rows)
+        remote(
+            codes.at[source], codes.at[source], code_send.at[0], code_recv.at[source], {"row": source}
+        ).wait_recv()
+        count(source)
+        return carry
+
+    lax.fori_loop(1, rows, count_peer, 0)
+
+    count_copies = [
+        remote(counts.at[d], counts.at[d], count_send.at[i], count_recv.at[d], {"depth": peer})
+        for i, peer in enumerate(depth_peers)
+    ]
+
+    for t in range(tables):
+        high, low = two_terms(table[t])
+        chosen = counts[d, :, t].reshape(rows * samples, rows_dev).astype(jnp.bfloat16)
+        part = matmul(chosen, high) + matmul(chosen, low)
+        partials[:, t] = part.reshape(rows, samples, features)
+
+    pool_copies = [
+        remote(partials.at[peer], pools.at[r], pool_send.at[i], pool_recv.at[r], {"row": peer})
+        for i, peer in enumerate(row_peers)
+    ]
+    for copy in pool_copies:
+        copy.start()
+    for copy in count_copies:
+        copy.start()
+    passed = [
+        remote(counts.at[d], counts.at[d], count_pass.at[0], count_recv.at[d], {"depth": partner})
+    ]
+    passed[0].start()
+    pools[r] = partials[r]
+
+    dequant = (dense_q[...].astype(jnp.float32) - 128.0) / 64.0
+    dense_vec = jnp.zeros((samples, features), jnp.float32)
+    for i in range(bottom_w.shape[0]):
+        dense_vec = dense_vec + dequant[:, i : i + 1] * bottom_w[i : i + 1, :]
+    label_col = jnp.zeros((samples, 1), jnp.float32)
+    sample_at = lax.broadcasted_iota(jnp.int32, (samples, 1), 0)
+    for b in range(samples):
+        label_col = jnp.where(sample_at == b, labels[b].astype(jnp.float32), label_col)
+    diagonal = lax.broadcasted_iota(jnp.int32, (rows_dev, rows_dev), 0) == lax.broadcasted_iota(
+        jnp.int32, (rows_dev, rows_dev), 1
+    )
+    for t in range(tables):
+        state_cols[t] = jnp.sum(
+            jnp.where(diagonal, accum[t : t + 1, :], 0.0), axis=1, keepdims=True
+        )
+
+    for peer in row_peers:
+        remote(
+            pools.at[peer], pools.at[peer], pool_send.at[0], pool_recv.at[peer], {"row": peer}
+        ).wait_recv()
+
+    bag_scale = float(bag_size) ** (-0.5)
+    width_scale = float(features) ** (-0.5)
+    vectors = [dense_vec] + [bag_scale * jnp.sum(pools[:, t], axis=0) for t in range(tables)]
+    pair_at = {}
+    for i in range(tables + 1):
+        for k in range(i + 1, tables + 1):
+            pair_at[i, k] = pair_at[k, i] = len(pair_at) // 2
+    mixed = []
+    for i in range(tables + 1):
+        terms = [top_w[pair_at[i, k]] * vectors[k] for k in range(tables + 1) if k != i]
+        mixed.append(functools.reduce(jnp.add, terms))
+    joined = functools.reduce(jnp.add, [vectors[i] * mixed[i] for i in range(tables + 1)])
+    logit = (0.5 * width_scale) * jnp.sum(joined, axis=1, keepdims=True)
+    coeff = (1.0 / (1.0 + jnp.exp(-logit)) - label_col) * (bag_scale * width_scale)
+    for t in range(tables):
+        grads[d, r, t] = coeff * mixed[1 + t]
+
+    grad_copies = []
+    for i, peer in enumerate(row_peers):
+        grad_copies.append(
+            remote(
+                grads.at[d, r], grads.at[d, r], grad_send.at[i], grad_recv.at[d, r], {"row": peer}
+            )
+        )
+
+    def spread(n, row):
+        made = [
+            remote(
+                grads.at[d, row],
+                grads.at[d, row],
+                grad_spread.at[n, i],
+                grad_recv.at[d, row],
+                {"depth": peer},
+            )
+            for i, peer in enumerate(depth_peers)
+        ]
+        made.append(pass_on(0, n, d, row))
+        for copy in made:
+            copy.start()
+        return made
+
+    def pass_on(m, n, depth, row):
+        return remote(
+            grads.at[depth, row],
+            grads.at[depth, row],
+            grad_pass.at[m, n],
+            grad_recv.at[depth, row],
+            {"depth": partner},
+        )
+
+    for copy in grad_copies:
+        copy.start()
+    grad_copies += spread(0, r)
+
+    eye = lax.broadcasted_iota(jnp.int32, (samples, samples), 0) == lax.broadcasted_iota(
+        jnp.int32, (samples, samples), 1
+    )
+    logits_out[...] = jnp.sum(jnp.where(eye, logit, 0.0), axis=0, keepdims=True)
+
+    for n, peer in enumerate(row_peers):
+        remote(
+            grads.at[d, peer], grads.at[d, peer], grad_send.at[0], grad_recv.at[d, peer], {"row": peer}
+        ).wait_recv()
+        grad_copies += spread(n + 1, peer)
+
+    for m, peer in enumerate(depth_peers):
+        remote(
+            counts.at[peer], counts.at[peer], count_send.at[0], count_recv.at[peer], {"depth": peer}
+        ).wait_recv()
+        copy = remote(
+            counts.at[peer],
+            counts.at[peer],
+            count_pass.at[m + 1],
+            count_recv.at[peer],
+            {"depth": partner},
+        )
+        copy.start()
+        passed.append(copy)
+
+    for n, row in enumerate([r] + row_peers):
+        for m, peer in enumerate(depth_peers):
+            remote(
+                grads.at[peer, row],
+                grads.at[peer, row],
+                grad_send.at[0],
+                grad_recv.at[peer, row],
+                {"depth": peer},
+            ).wait_recv()
+            copy = pass_on(m + 1, n, peer, row)
+            copy.start()
+            grad_copies.append(copy)
+
+    for peer in partner_side:
+        remote(
+            counts.at[peer], counts.at[peer], count_send.at[0], count_recv.at[peer], {"depth": partner}
+        ).wait_recv()
+    batch = depths * rows * samples
+    for t in range(tables):
+        weights[t] = counts[:, :, t].reshape(batch, rows_dev).T.astype(jnp.bfloat16)
+
+    for row in [r] + row_peers:
+        for peer in partner_side:
+            remote(
+                grads.at[peer, row],
+                grads.at[peer, row],
+                grad_send.at[0],
+                grad_recv.at[peer, row],
+                {"depth": partner},
+            ).wait_recv()
+
+    for t in range(tables):
+        high, low = two_terms(grads[:, :, t].reshape(batch, features))
+        row_grad = matmul(weights[t], high) + matmul(weights[t], low)
+        state = state_cols[t] + jnp.sum(row_grad * row_grad, axis=1, keepdims=True) / features
+        new_table[t] = table[t] - row_grad * (LEARN_RATE / (jnp.sqrt(state) + EPSILON))
+        new_accum[t : t + 1, :] = jnp.sum(jnp.where(diagonal, state, 0.0), axis=0, keepdims=True)
+
+    for copy in code_copies + count_copies + passed + pool_copies + grad_copies:
+        copy.wait_send()
+
+
+def shards_small(table, accum, owner, local_row, lengths, dense_q, labels, bottom_w, top_w):
+    tables, rows_dev, features = table.shape
+    samples, bag_size = (owner.shape[0], owner.shape[2])
+    rows = lax.axis_size("row")
+    depths = lax.axis_size("depth")
+    half = depths // 2
+    f32 = jnp.float32
+    dma = pltpu.SemaphoreType.DMA
+    vmem = pl.BlockSpec(memory_space=pltpu.VMEM)
+    smem = pl.BlockSpec(memory_space=pltpu.SMEM)
+    block = (tables, samples, features)
+    new_table, new_accum, logits = pl.pallas_call(
+        step_kernel,
+        out_shape=[
+            jax.ShapeDtypeStruct(table.shape, f32),
+            jax.ShapeDtypeStruct(accum.shape, f32),
+            jax.ShapeDtypeStruct((1, samples), f32),
+        ],
+        in_specs=[vmem, vmem, vmem, vmem, vmem, vmem, smem, vmem, smem],
+        out_specs=[vmem, vmem, vmem],
+        scratch_shapes=[
+            pltpu.VMEM((rows, tables // 2, samples, 2 * bag_size), jnp.int32),
+            pltpu.VMEM((depths, rows, tables, samples, rows_dev), f32),
+            pltpu.VMEM((rows,) + block, f32),
+            pltpu.VMEM((rows,) + block, f32),
+            pltpu.VMEM((depths, rows) + block, f32),
+            pltpu.VMEM((tables, rows_dev, depths * rows * samples), jnp.bfloat16),
+            pltpu.VMEM((tables, rows_dev, 1), f32),
+            dma((rows - 1,)),
+            dma((rows,)),
+            dma((half - 1,)),
+            dma((half,)),
+            dma((depths,)),
+            dma((rows - 1,)),
+            dma((rows,)),
+            dma((rows - 1,)),
+            dma((rows, half - 1)),
+            dma((half, rows)),
+            dma((depths, rows)),
+        ],
+        compiler_params=pltpu.CompilerParams(
+            collective_id=0, has_side_effects=True, vmem_limit_bytes=32 * 1024 * 1024
+        ),
+    )(
+        table,
+        accum,
+        owner.reshape(samples, tables, bag_size),
+        local_row,
+        lengths,
+        dense_q,
+        labels,
+        bottom_w,
+        top_w,
+    )
+    return new_table, new_accum, logits.reshape(samples)
+
+
+def by_size(table, *rest):
+    tables, _, features = table.shape
+    samples = rest[1].shape[0]
+    devices = lax.axis_size("row") * lax.axis_size("depth")
+    gathered = devices * samples * tables * features * 4
+    if gathered <= 4 * 1024 * 1024:
+        return shards_small(table, *rest)
+    return shards_large(table, *rest)
+
+
 def solution(mesh):
     in_specs = (
         P(None, "row", None),
@@ -108,4 +464,4 @@
         P(),
     )
     out_specs = (P(None, "row", None), P(None, "row"), P(("row", "depth")))
-    return jax.shard_map(shards, mesh=mesh, in_specs=in_specs, out_specs=out_specs, check_vma=False)
+    return jax.shard_map(by_size, mesh=mesh, in_specs=in_specs, out_specs=out_specs, check_vma=False)

time: 202 us -> 35.2 us (0.17)
  waiting for transfers between devices: 65.7 us -> 0 us
  other arithmetic: 61.6 us -> 0 us
  Pallas kernels: 0 us -> 27.1 us
  local copies, waits for them, and re-layouts: 31.7 us -> 6.92 us
  between operations: 14.2 us -> 0.68 us
  blocking collectives: 11.1 us -> 0 us
  starting transfers between devices: 9.87 us -> 0 us
  matrix products: 5.84 us -> 0 us
    psum x1 -> x0, waiting for transfers between devices: 60.9 us -> none  [shards(): summed = lax.psum(row_grad, 'depth')]
    scatter-add x1 -> x0, other arithmetic: 53.2 us -> none  [shards(): row_grad = jnp.zeros((row_span, features), jnp.float32).at[flat_rows.resh...]
    pallas_call x0 -> x1, Pallas kernels: none -> 27.1 us  [shards_small(): pl.pallas_call(step_kernel, out_shape=[jax.ShapeDtypeStruct(table.shape,...]
    gather x1 -> x0, local copies, waits for them, and re-layouts: 16.1 us -> none  [shards(): picked = flat_table[flat_rows]]
    scatter x3 -> x0, local copies, waits for them, and re-layouts: 12.1 us -> none  [the longest x1 8.62 us: shards(): outgoing = jnp.full((row_devices * capacity,), -1, jnp.int32).at[owner_of...]
    all_gather x1 -> x0, blocking collectives: 11.1 us -> none  [shards(): piece = lax.all_gather(pooled_grad, 'row', axis=0, tiled=True)]
    all_to_all x2 -> x0, starting transfers between devices: 9.87 us -> none  [the longest x1 5.42 us: shards(): lax.all_to_all(outgoing.reshape(row_devices, capacity), 'row', split_axis...]
    dot_general x4 -> x0, matrix products: 5.84 us -> none  [the longest x1 4.51 us: shards(): jnp.einsum('sbc,scw->sbw', choose, picked, precision=lax.Precision.HIGHEST)]
  transfers between devices with their start and end apart: 3 -> 0, of which waited for: 3 -> 0; matrix products, arithmetic and copies ran while one was open for 2% -> 0% of each run, Pallas kernels for 0% -> 0%
where the time goes in v1:
time: 35.2 us; the launch traced here: 34.7 us
  Pallas kernels  27.1 us (77%)
  local copies, waits for them, and re-layouts  6.92 us (20%)
  between operations  0.68 us (2%)
    pallas_call x1, Pallas kernels, shards_small(): pl.pallas_call(step_kernel, out_shape=[jax.ShapeDtypeStruct(table.shape,...  27.1 us
    unnamed x20, local copies, waits for them, and re-layouts  6.92 us

profile of v1, /device:TPU:1, one launch (start us, length us, event | category | flops | bytes accessed | tf_op | source)
XLA Modules:
  0.0 34.7 jit_solution(5850615760884268785)
XLA Ops:
  0.6 0.0 copy-start.4
  0.6 0.0 copy-start.6
  0.7 0.0 copy-start.7
  0.7 0.8 %copy.12.lengths = s32[8,4]{1,0:T(8,128)S(1)} copy(s32[8,4]{0,1:T(4,128)} %param.13) | data formatting | bytes 256 | tf_op args[4]
  1.4 0.0 copy-done.4
  1.4 0.0 copy-done.6
  1.4 0.0 copy-done.7
  1.4 0.0 copy-start
  1.5 1.2 %copy-done = f32[4,256,256]{2,1,0:T(8,128)S(1)} copy-done((f32[4,256,256]{2,1,0:T(8,128)S(1)}, f32[4,256,256]{2,1,0:T(8,128)}, u32[]{:S(2)}) %copy-start) | copy-done | bytes 1048600
  2.7 0.0 copy-start.1
  2.7 0.7 %copy-done.1 = s32[8,4,64,1]{2,3,1,0:T(1,128)S(1)} copy-done((s32[8,4,64,1]{2,3,1,0:T(1,128)S(1)}, s32[8,4,64,1]{2,3,1,0:T(1,128)}, u32[]{:S(2)}) %copy-start.1) | copy-done | bytes 8216
  3.4 0.0 copy-start.2
  3.4 0.7 %copy-done.2 = s32[8,4,64]{2,1,0:T(4,128)S(1)} copy-done((s32[8,4,64]{2,1,0:T(4,128)S(1)}, s32[8,4,64]{2,1,0:T(4,128)}, u32[]{:S(2)}) %copy-start.2) | copy-done | bytes 8216
  4.1 0.0 copy-start.3
  4.1 0.7 %copy-done.3 = f32[13,256]{1,0:T(8,128)S(1)} copy-done((f32[13,256]{1,0:T(8,128)S(1)}, f32[13,256]{1,0:T(8,128)}, u32[]{:S(2)}) %copy-start.3) | copy-done | bytes 13336
  4.8 0.0 copy-start.5
  4.8 0.7 %copy-done.5 = s32[8,13]{1,0:T(8,128)S(1)} copy-done((s32[8,13]{1,0:T(8,128)S(1)}, s32[8,13]{1,0:T(8,128)}, u32[]{:S(2)}) %copy-start.5) | copy-done | bytes 440
  5.5 27.1 %shard_map.112 = (f32[4,256,256]{2,1,0:T(8,128)S(1)}, f32[4,256]{1,0:T(4,128)S(1)}, f32[1,8]{1,0:T(1,128)S(1)}) custom-call(f32[4,256,256]{2,1,0:T(8,128)S(1)} %copy-done, f32[4,256]{1,0:T(4,128)S(1)} %copy-done.4, s32[8,4,64]{2,1,0:T(4,128)S(1)} %bitcast.2, s32[8,4,64]{2,1,0:T(4,128)S(1)} %copy-done.2, s32[8,4]{1,0:T(8,128)S(1)} %copy.12.lengths, ...), custom_call_target="tpu_custom_call" | custom-call | tf_op jit(solution)/shard_map/pallas_call | solution.py:398
  32.6 1.0 %copy.16 = f32[4,256,256]{2,1,0:T(8,128)} copy(f32[4,256,256]{2,1,0:T(8,128)S(1)} %get-tuple-element.12) | data formatting | bytes 2097152
  33.6 0.6 %copy.17 = f32[4,256]{1,0:T(4,128)} copy(f32[4,256]{1,0:T(4,128)S(1)} %get-tuple-element.13) | data formatting | bytes 8192
  34.2 0.5 %copy.18 = f32[8]{0:T(128)} copy(f32[8]{0:T(128)S(1)} %bitcast.3) | data formatting | bytes 64
Async XLA Ops:
  0.6 0.8 %copy-start.4 = (f32[4,256]{1,0:T(4,128)S(1)}, f32[4,256]{1,0:T(4,128)}, u32[]{:S(2)}) copy-start(f32[4,256]{1,0:T(4,128)} %accum.1) | copy-start | bytes 12292
  0.6 0.8 %copy-start.6 = (s32[8]{0:T(128)S(1)}, s32[8]{0:T(128)}, u32[]{:S(2)}) copy-start(s32[8]{0:T(128)} %labels.1) | copy-start | bytes 100
  0.7 0.8 %copy-start.7 = (f32[10]{0:T(128)S(1)}, f32[10]{0:T(128)}, u32[]{:S(2)}) copy-start(f32[10]{0:T(128)} %top_w.1) | copy-start | bytes 124
  1.4 1.2 %copy-start = (f32[4,256,256]{2,1,0:T(8,128)S(1)}, f32[4,256,256]{2,1,0:T(8,128)}, u32[]{:S(2)}) copy-start(f32[4,256,256]{2,1,0:T(8,128)} %table.1) | copy-start | bytes 3145732
  2.7 0.7 %copy-start.1 = (s32[8,4,64,1]{2,3,1,0:T(1,128)S(1)}, s32[8,4,64,1]{2,3,1,0:T(1,128)}, u32[]{:S(2)}) copy-start(s32[8,4,64,1]{2,3,1,0:T(1,128)} %param.11) | copy-start | bytes 24580
  3.4 0.7 %copy-start.2 = (s32[8,4,64]{2,1,0:T(4,128)S(1)}, s32[8,4,64]{2,1,0:T(4,128)}, u32[]{:S(2)}) copy-start(s32[8,4,64]{2,1,0:T(4,128)} %local_row.1) | copy-start | bytes 24580
  4.1 0.7 %copy-start.3 = (f32[13,256]{1,0:T(8,128)S(1)}, f32[13,256]{1,0:T(8,128)}, u32[]{:S(2)}) copy-start(f32[13,256]{1,0:T(8,128)} %bottom_w.1) | copy-start | bytes 39940
  4.8 0.7 %copy-start.5 = (s32[8,13]{1,0:T(8,128)S(1)}, s32[8,13]{1,0:T(8,128)}, u32[]{:S(2)}) copy-start(s32[8,13]{1,0:T(8,128)} %dense_q.1) | copy-start | bytes 1252

commit v2 on v1

--- a/solution.py
+++ b/solution.py
@@ -120,6 +120,18 @@
 
 
 def step_kernel(
+    table_in,
+    accum_in,
+    owner_in,
+    local_in,
+    lengths_in,
+    dense_in,
+    labels_in,
+    bottom_in,
+    top_in,
+    new_table,
+    new_accum,
+    logits_out,
     table,
     accum,
     owner,
@@ -129,9 +141,9 @@
     labels,
     bottom_w,
     top_w,
-    new_table,
-    new_accum,
-    logits_out,
+    table_high,
+    table_low,
+    fetch,
     codes,
     counts,
     partials,
@@ -173,10 +185,35 @@
             barrier, inc=1, device_id={"depth": peer}, device_id_type=pl.DeviceIdType.MESH
         )
 
-    slot_at = lax.broadcasted_iota(jnp.int32, (samples, bag_size), 1)
+    fetches = [
+        pltpu.make_async_copy(source, target, fetch.at[i])
+        for i, (source, target) in enumerate(
+            [
+                (owner_in, owner),
+                (local_in, local_row),
+                (lengths_in, lengths),
+                (table_in, table),
+                (accum_in, accum),
+                (dense_in, dense_q),
+                (labels_in, labels),
+                (bottom_in, bottom_w),
+                (top_in, top_w),
+            ]
+        )
+    ]
+    for copy in fetches:
+        copy.start()
+    eye = lax.broadcasted_iota(jnp.int32, (samples, samples), 0) == lax.broadcasted_iota(
+        jnp.int32, (samples, samples), 1
+    )
+    for copy in fetches[:3]:
+        copy.wait()
+
+    slot_at = lax.broadcasted_iota(jnp.int32, (samples, bag_size), 1).astype(jnp.float32)
+    lengths_f = lengths[...].astype(jnp.float32)
     mine = []
     for t in range(tables):
-        live = slot_at < lengths[:, t : t + 1]
+        live = slot_at < jnp.sum(jnp.where(eye, lengths_f[t : t + 1, :], 0.0), axis=1, keepdims=True)
         mine.append(jnp.where(live, owner[:, t, :] * rows_dev + local_row[:, t, :], -1))
     for p in range(tables // 2):
         codes[r, p] = jnp.concatenate([mine[2 * p], mine[2 * p + 1]], axis=1)
@@ -205,7 +242,21 @@
 
         lax.fori_loop(0, tables // 2, pair, 0)
 
+    def pool_copy(k, source):
+        return remote(
+            partials.at[source], pools.at[r], pool_send.at[k], pool_recv.at[r], {"row": source}
+        )
+
+    def pool(source, target):
+        for t in range(tables):
+            chosen = counts[d, source, t].astype(jnp.bfloat16)
+            target[source, t] = matmul(chosen, table_high[t]) + matmul(chosen, table_low[t])
+
     count(r)
+    for copy in fetches[3:]:
+        copy.wait()
+    for t in range(tables):
+        table_high[t], table_low[t] = two_terms(table[t])
 
     def count_peer(k, carry):
         source = lax.rem(r + k, rows)
@@ -213,6 +264,8 @@
             codes.at[source], codes.at[source], code_send.at[0], code_recv.at[source], {"row": source}
         ).wait_recv()
         count(source)
+        pool(source, partials)
+        pool_copy(k - 1, source).start()
         return carry
 
     lax.fori_loop(1, rows, count_peer, 0)
@@ -222,25 +275,14 @@
         for i, peer in enumerate(depth_peers)
     ]
 
-    for t in range(tables):
-        high, low = two_terms(table[t])
-        chosen = counts[d, :, t].reshape(rows * samples, rows_dev).astype(jnp.bfloat16)
-        part = matmul(chosen, high) + matmul(chosen, low)
-        partials[:, t] = part.reshape(rows, samples, features)
-
-    pool_copies = [
-        remote(partials.at[peer], pools.at[r], pool_send.at[i], pool_recv.at[r], {"row": peer})
-        for i, peer in enumerate(row_peers)
-    ]
-    for copy in pool_copies:
-        copy.start()
+    pool_copies = [pool_copy(i, peer) for i, peer in enumerate(row_peers)]
     for copy in count_copies:
         copy.start()
     passed = [
         remote(counts.at[d], counts.at[d], count_pass.at[0], count_recv.at[d], {"depth": partner})
     ]
     passed[0].start()
-    pools[r] = partials[r]
+    pool(r, pools)
 
     dequant = (dense_q[...].astype(jnp.float32) - 128.0) / 64.0
     dense_vec = jnp.zeros((samples, features), jnp.float32)
@@ -317,9 +359,6 @@
         copy.start()
     grad_copies += spread(0, r)
 
-    eye = lax.broadcasted_iota(jnp.int32, (samples, samples), 0) == lax.broadcasted_iota(
-        jnp.int32, (samples, samples), 1
-    )
     logits_out[...] = jnp.sum(jnp.where(eye, logit, 0.0), axis=0, keepdims=True)
 
     for n, peer in enumerate(row_peers):
@@ -393,7 +432,8 @@
     f32 = jnp.float32
     dma = pltpu.SemaphoreType.DMA
     vmem = pl.BlockSpec(memory_space=pltpu.VMEM)
-    smem = pl.BlockSpec(memory_space=pltpu.SMEM)
+    hbm = pl.BlockSpec(memory_space=pltpu.HBM)
+    i32 = jnp.int32
     block = (tables, samples, features)
     new_table, new_accum, logits = pl.pallas_call(
         step_kernel,
@@ -402,9 +442,21 @@
             jax.ShapeDtypeStruct(accum.shape, f32),
             jax.ShapeDtypeStruct((1, samples), f32),
         ],
-        in_specs=[vmem, vmem, vmem, vmem, vmem, vmem, smem, vmem, smem],
+        in_specs=[hbm] * 9,
         out_specs=[vmem, vmem, vmem],
         scratch_shapes=[
+            pltpu.VMEM(table.shape, f32),
+            pltpu.VMEM(accum.shape, f32),
+            pltpu.VMEM((samples, tables, bag_size), i32),
+            pltpu.VMEM(local_row.shape, i32),
+            pltpu.VMEM((tables, samples), i32),
+            pltpu.VMEM(dense_q.shape, i32),
+            pltpu.SMEM(labels.shape, i32),
+            pltpu.VMEM(bottom_w.shape, f32),
+            pltpu.SMEM(top_w.shape, f32),
+            pltpu.VMEM(table.shape, jnp.bfloat16),
+            pltpu.VMEM(table.shape, jnp.bfloat16),
+            dma((9,)),
             pltpu.VMEM((rows, tables // 2, samples, 2 * bag_size), jnp.int32),
             pltpu.VMEM((depths, rows, tables, samples, rows_dev), f32),
             pltpu.VMEM((rows,) + block, f32),
@@ -425,14 +477,14 @@
             dma((depths, rows)),
         ],
         compiler_params=pltpu.CompilerParams(
-            collective_id=0, has_side_effects=True, vmem_limit_bytes=32 * 1024 * 1024
+            collective_id=0, has_side_effects=True, vmem_limit_bytes=63 * 1024 * 1024
         ),
     )(
         table,
         accum,
         owner.reshape(samples, tables, bag_size),
         local_row,
-        lengths,
+        lengths.T,
         dense_q,
         labels,
         bottom_w,

time: 35.2 us -> 31.2 us (0.89)
  local copies, waits for them, and re-layouts: 6.92 us -> 3.4 us
    unnamed x20 -> x7, local copies, waits for them, and re-layouts: 6.92 us -> 3.4 us
where the time goes in v2:
time: 31.2 us; the launch traced here: 31 us
  Pallas kernels  26.9 us (86%)
  local copies, waits for them, and re-layouts  3.4 us (11%)
  between operations  0.65 us (2%)
    pallas_call x1, Pallas kernels, shards_small(): pl.pallas_call(step_kernel, out_shape=[jax.ShapeDtypeStruct(table.shape,...  26.9 us
    unnamed x7, local copies, waits for them, and re-layouts  3.4 us

profile of v2, /device:TPU:1, one launch (start us, length us, event | category | flops | bytes accessed | tf_op | source)
XLA Modules:
  0.0 31.0 jit_solution(4886771346515769527)
XLA Ops:
  0.6 26.9 %shard_map.112 = (f32[4,256,256]{2,1,0:T(8,128)}, f32[4,256]{1,0:T(4,128)}, f32[1,8]{1,0:T(1,128)}) custom-call(f32[4,256,256]{2,1,0:T(8,128)} %table_in.1, f32[4,256]{1,0:T(4,128)} %accum_in.1, s32[8,4,64]{2,1,0:T(4,128)} %bitcast.3, s32[8,4,64]{2,1,0:T(4,128)} %local_in.1, s32[4,8]{1,0:T(4,128)} %bitcast.4, s32[8,13]{1,0:T(8,128)} %dense_in.1, ...), custom_call_target="tpu_custom_call" | custom-call | tf_op jit(solution)/shard_map/pallas_call | solution.py:438
  27.5 0.0 copy-start
  27.6 2.3 %copy.15 = f32[4,256,256]{2,1,0:T(8,128)} copy(f32[4,256,256]{2,1,0:T(8,128)} %get-tuple-element.12) | data formatting | bytes 2097152
  29.8 0.0 copy-done
  29.8 0.0 copy-start.1
  29.8 0.6 %copy.16 = f32[4,256]{1,0:T(4,128)} copy(f32[4,256]{1,0:T(4,128)S(1)} %copy-done) | data formatting | bytes 8192
  30.4 0.0 copy-done.1
  30.4 0.5 %copy.17 = f32[8]{0:T(128)} copy(f32[8]{0:T(128)S(1)} %bitcast.5) | data formatting | bytes 64
Async XLA Ops:
  27.5 2.3 %copy-start = (f32[4,256]{1,0:T(4,128)S(1)}, f32[4,256]{1,0:T(4,128)}, u32[]{:S(2)}) copy-start(f32[4,256]{1,0:T(4,128)} %get-tuple-element.13) | copy-start | bytes 12292
  29.8 0.6 %copy-start.1 = (f32[1,8]{1,0:T(1,128)S(1)}, f32[1,8]{1,0:T(1,128)}, u32[]{:S(2)}) copy-start(f32[1,8]{1,0:T(1,128)} %get-tuple-element.8) | copy-start | bytes 100

commit v3 on v2

--- a/solution.py
+++ b/solution.py
@@ -121,7 +121,6 @@
 
 def step_kernel(
     table_in,
-    accum_in,
     owner_in,
     local_in,
     lengths_in,
@@ -129,11 +128,9 @@
     labels_in,
     bottom_in,
     top_in,
-    new_table,
-    new_accum,
+    row_grad_out,
     logits_out,
     table,
-    accum,
     owner,
     local_row,
     lengths,
@@ -150,7 +147,8 @@
     pools,
     grads,
     weights,
-    state_cols,
+    row_grad,
+    store,
     code_send,
     code_recv,
     count_send,
@@ -193,7 +191,6 @@
                 (local_in, local_row),
                 (lengths_in, lengths),
                 (table_in, table),
-                (accum_in, accum),
                 (dense_in, dense_q),
                 (labels_in, labels),
                 (bottom_in, bottom_w),
@@ -217,15 +214,6 @@
         mine.append(jnp.where(live, owner[:, t, :] * rows_dev + local_row[:, t, :], -1))
     for p in range(tables // 2):
         codes[r, p] = jnp.concatenate([mine[2 * p], mine[2 * p + 1]], axis=1)
-
-    pl.semaphore_wait(barrier, rows - 1 + half)
-
-    code_copies = [
-        remote(codes.at[r], codes.at[r], code_send.at[i], code_recv.at[r], {"row": peer})
-        for i, peer in enumerate(row_peers)
-    ]
-    for copy in code_copies:
-        copy.start()
 
     row_at = lax.broadcasted_iota(jnp.int32, (samples, rows_dev), 1)
 
@@ -258,6 +246,15 @@
     for t in range(tables):
         table_high[t], table_low[t] = two_terms(table[t])
 
+    pl.semaphore_wait(barrier, rows - 1 + half)
+
+    code_copies = [
+        remote(codes.at[r], codes.at[r], code_send.at[i], code_recv.at[r], {"row": peer})
+        for i, peer in enumerate(row_peers)
+    ]
+    for copy in code_copies:
+        copy.start()
+
     def count_peer(k, carry):
         source = lax.rem(r + k, rows)
         remote(
@@ -292,14 +289,6 @@
     sample_at = lax.broadcasted_iota(jnp.int32, (samples, 1), 0)
     for b in range(samples):
         label_col = jnp.where(sample_at == b, labels[b].astype(jnp.float32), label_col)
-    diagonal = lax.broadcasted_iota(jnp.int32, (rows_dev, rows_dev), 0) == lax.broadcasted_iota(
-        jnp.int32, (rows_dev, rows_dev), 1
-    )
-    for t in range(tables):
-        state_cols[t] = jnp.sum(
-            jnp.where(diagonal, accum[t : t + 1, :], 0.0), axis=1, keepdims=True
-        )
-
     for peer in row_peers:
         remote(
             pools.at[peer], pools.at[peer], pool_send.at[0], pool_recv.at[peer], {"row": peer}
@@ -414,13 +403,74 @@
 
     for t in range(tables):
         high, low = two_terms(grads[:, :, t].reshape(batch, features))
-        row_grad = matmul(weights[t], high) + matmul(weights[t], low)
-        state = state_cols[t] + jnp.sum(row_grad * row_grad, axis=1, keepdims=True) / features
-        new_table[t] = table[t] - row_grad * (LEARN_RATE / (jnp.sqrt(state) + EPSILON))
-        new_accum[t : t + 1, :] = jnp.sum(jnp.where(diagonal, state, 0.0), axis=0, keepdims=True)
-
+        row_grad[t] = matmul(weights[t], high) + matmul(weights[t], low)
+        pltpu.make_async_copy(row_grad.at[t], row_grad_out.at[t], store.at[t]).start()
+
+    for t in range(tables):
+        pltpu.make_async_copy(row_grad.at[t], row_grad_out.at[t], store.at[t]).wait()
     for copy in code_copies + count_copies + passed + pool_copies + grad_copies:
         copy.wait_send()
+
+
+def update_kernel(
+    grad_in,
+    table_in,
+    accum_in,
+    logits_in,
+    new_table,
+    new_accum,
+    logits_out,
+    grad,
+    table,
+    accum,
+    result,
+    state_rows,
+    fetch,
+    store,
+):
+    tables, rows_dev, features = table.shape
+    first = [
+        pltpu.make_async_copy(accum_in, accum, fetch.at[2 * tables]),
+        pltpu.make_async_copy(logits_in, logits_out, fetch.at[2 * tables + 1]),
+    ]
+    blocks = [
+        (
+            pltpu.make_async_copy(grad_in.at[t], grad.at[t], fetch.at[2 * t]),
+            pltpu.make_async_copy(table_in.at[t], table.at[t], fetch.at[2 * t + 1]),
+        )
+        for t in range(tables)
+    ]
+    stores = [
+        pltpu.make_async_copy(result.at[t], new_table.at[t], store.at[t]) for t in range(tables)
+    ]
+    stores.append(pltpu.make_async_copy(state_rows, new_accum, store.at[tables]))
+    for copy in first:
+        copy.start()
+    for pair in blocks:
+        for copy in pair:
+            copy.start()
+    diagonal = lax.broadcasted_iota(jnp.int32, (rows_dev, rows_dev), 0) == lax.broadcasted_iota(
+        jnp.int32, (rows_dev, rows_dev), 1
+    )
+    first[0].wait()
+    before = [
+        jnp.sum(jnp.where(diagonal, accum[t : t + 1, :], 0.0), axis=1, keepdims=True)
+        for t in range(tables)
+    ]
+    for t in range(tables):
+        for copy in blocks[t]:
+            copy.wait()
+        row_grad = grad[t]
+        state = before[t] + jnp.sum(row_grad * row_grad, axis=1, keepdims=True) / features
+        result[t] = table[t] - row_grad * (LEARN_RATE / (jnp.sqrt(state) + EPSILON))
+        stores[t].start()
+        state_rows[t : t + 1, :] = jnp.sum(
+            jnp.where(diagonal, state, 0.0), axis=0, keepdims=True
+        )
+    stores[tables].start()
+    first[1].wait()
+    for copy in stores:
+        copy.wait()
 
 
 def shards_small(table, accum, owner, local_row, lengths, dense_q, labels, bottom_w, top_w):
@@ -435,18 +485,17 @@
     hbm = pl.BlockSpec(memory_space=pltpu.HBM)
     i32 = jnp.int32
     block = (tables, samples, features)
-    new_table, new_accum, logits = pl.pallas_call(
+    params = dict(has_side_effects=True, vmem_limit_bytes=63 * 1024 * 1024)
+    row_grad, logits = pl.pallas_call(
         step_kernel,
         out_shape=[
             jax.ShapeDtypeStruct(table.shape, f32),
-            jax.ShapeDtypeStruct(accum.shape, f32),
             jax.ShapeDtypeStruct((1, samples), f32),
         ],
-        in_specs=[hbm] * 9,
-        out_specs=[vmem, vmem, vmem],
+        in_specs=[hbm] * 8,
+        out_specs=[hbm, vmem],
         scratch_shapes=[
             pltpu.VMEM(table.shape, f32),
-            pltpu.VMEM(accum.shape, f32),
             pltpu.VMEM((samples, tables, bag_size), i32),
             pltpu.VMEM(local_row.shape, i32),
             pltpu.VMEM((tables, samples), i32),
@@ -456,14 +505,15 @@
             pltpu.SMEM(top_w.shape, f32),
             pltpu.VMEM(table.shape, jnp.bfloat16),
             pltpu.VMEM(table.shape, jnp.bfloat16),
-            dma((9,)),
+            dma((8,)),
             pltpu.VMEM((rows, tables // 2, samples, 2 * bag_size), jnp.int32),
             pltpu.VMEM((depths, rows, tables, samples, rows_dev), f32),
             pltpu.VMEM((rows,) + block, f32),
             pltpu.VMEM((rows,) + block, f32),
             pltpu.VMEM((depths, rows) + block, f32),
             pltpu.VMEM((tables, rows_dev, depths * rows * samples), jnp.bfloat16),
-            pltpu.VMEM((tables, rows_dev, 1), f32),
+            pltpu.VMEM(table.shape, f32),
+            dma((tables,)),
             dma((rows - 1,)),
             dma((rows,)),
             dma((half - 1,)),
@@ -476,12 +526,9 @@
             dma((half, rows)),
             dma((depths, rows)),
         ],
-        compiler_params=pltpu.CompilerParams(
-            collective_id=0, has_side_effects=True, vmem_limit_bytes=63 * 1024 * 1024
-        ),
+        compiler_params=pltpu.CompilerParams(collective_id=0, **params),
     )(
         table,
-        accum,
         owner.reshape(samples, tables, bag_size),
         local_row,
         lengths.T,
@@ -490,6 +537,26 @@
         bottom_w,
         top_w,
     )
+    new_table, new_accum, logits = pl.pallas_call(
+        update_kernel,
+        out_shape=[
+            jax.ShapeDtypeStruct(table.shape, f32),
+            jax.ShapeDtypeStruct(accum.shape, f32),
+            jax.ShapeDtypeStruct(logits.shape, f32),
+        ],
+        in_specs=[hbm] * 4,
+        out_specs=[hbm] * 3,
+        scratch_shapes=[
+            pltpu.VMEM(table.shape, f32),
+            pltpu.VMEM(table.shape, f32),
+            pltpu.VMEM(accum.shape, f32),
+            pltpu.VMEM(table.shape, f32),
+            pltpu.VMEM(accum.shape, f32),
+            dma((2 * tables + 2,)),
+            dma((tables + 1,)),
+        ],
+        compiler_params=pltpu.CompilerParams(vmem_limit_bytes=63 * 1024 * 1024),
+    )(row_grad, table, accum, logits)
     return new_table, new_accum, logits.reshape(samples)
 
 

time: 31.2 us -> 30.3 us (0.971)
  local copies, waits for them, and re-layouts: 3.4 us -> 0 us
  Pallas kernels: 26.9 us -> 29.4 us
    unnamed x7 -> x0, local copies, waits for them, and re-layouts: 3.4 us -> none
    pallas_call x0 -> x1, Pallas kernels: none -> 2.56 us  [shards_small(): pl.pallas_call(update_kernel, out_shape=[jax.ShapeDtypeStruct(table.shape...]
where the time goes in v3:
time: 30.3 us; the launch traced here: 30.1 us
  Pallas kernels  29.4 us (97%)
  between operations  0.64 us (2%)
    pallas_call x1, Pallas kernels, shards_small(): pl.pallas_call(step_kernel, out_shape=[jax.ShapeDtypeStruct(table.shape,...  26.9 us
    pallas_call x1, Pallas kernels, shards_small(): pl.pallas_call(update_kernel, out_shape=[jax.ShapeDtypeStruct(table.shape...  2.56 us

profile of v3, /device:TPU:1, one launch (start us, length us, event | category | flops | bytes accessed | tf_op | source)
XLA Modules:
  0.0 30.1 jit_solution(5905832939668508583)
XLA Ops:
  0.6 26.9 %shard_map.112 = (f32[4,256,256]{2,1,0:T(8,128)}, f32[1,8]{1,0:T(1,128)}) custom-call(f32[4,256,256]{2,1,0:T(8,128)} %table_in.3, s32[8,4,64]{2,1,0:T(4,128)} %bitcast.3, s32[8,4,64]{2,1,0:T(4,128)} %local_in.1, s32[4,8]{1,0:T(4,128)} %bitcast.4, s32[8,13]{1,0:T(8,128)} %dense_in.1, s32[8]{0:T(128)} %labels_in.1, f32[13,256]{1,0:T(8,128)} %bottom_in.1, f32[10]{0:T(128)} %top_in.1), custom_call_target="tpu_custom_call" | custom-call | tf_op jit(solution)/shard_map/pallas_call | solution.py:489
  27.5 2.6 %shard_map.113 = (f32[4,256,256]{2,1,0:T(8,128)}, f32[4,256]{1,0:T(4,128)}, f32[1,8]{1,0:T(1,128)}) custom-call(f32[4,256,256]{2,1,0:T(8,128)} %get-tuple-element.8.grad_in, f32[4,256,256]{2,1,0:T(8,128)} %table_in.3, f32[4,256]{1,0:T(4,128)} %accum_in.1, f32[1,8]{1,0:T(1,128)} %get-tuple-element.9.logits_in), custom_call_target="tpu_custom_call" | custom-call | tf_op jit(solution)/shard_map/pallas_call | solution.py:540

commit v4 on v3

--- a/solution.py
+++ b/solution.py
@@ -148,6 +148,7 @@
     grads,
     weights,
     row_grad,
+    logit_row,
     store,
     code_send,
     code_recv,
@@ -348,7 +349,9 @@
         copy.start()
     grad_copies += spread(0, r)
 
-    logits_out[...] = jnp.sum(jnp.where(eye, logit, 0.0), axis=0, keepdims=True)
+    logit_row[...] = jnp.sum(jnp.where(eye, logit, 0.0), axis=0, keepdims=True)
+    logits_copy = pltpu.make_async_copy(logit_row, logits_out, store.at[tables])
+    logits_copy.start()
 
     for n, peer in enumerate(row_peers):
         remote(
@@ -391,6 +394,9 @@
     for t in range(tables):
         weights[t] = counts[:, :, t].reshape(batch, rows_dev).T.astype(jnp.bfloat16)
 
+    for copy in code_copies + count_copies + passed + pool_copies:
+        copy.wait_send()
+    logits_copy.wait()
     for row in [r] + row_peers:
         for peer in partner_side:
             remote(
@@ -406,10 +412,10 @@
         row_grad[t] = matmul(weights[t], high) + matmul(weights[t], low)
         pltpu.make_async_copy(row_grad.at[t], row_grad_out.at[t], store.at[t]).start()
 
+    for copy in grad_copies:
+        copy.wait_send()
     for t in range(tables):
         pltpu.make_async_copy(row_grad.at[t], row_grad_out.at[t], store.at[t]).wait()
-    for copy in code_copies + count_copies + passed + pool_copies + grad_copies:
-        copy.wait_send()
 
 
 def update_kernel(
@@ -481,7 +487,6 @@
     half = depths // 2
     f32 = jnp.float32
     dma = pltpu.SemaphoreType.DMA
-    vmem = pl.BlockSpec(memory_space=pltpu.VMEM)
     hbm = pl.BlockSpec(memory_space=pltpu.HBM)
     i32 = jnp.int32
     block = (tables, samples, features)
@@ -493,7 +498,7 @@
             jax.ShapeDtypeStruct((1, samples), f32),
         ],
         in_specs=[hbm] * 8,
-        out_specs=[hbm, vmem],
+        out_specs=[hbm, hbm],
         scratch_shapes=[
             pltpu.VMEM(table.shape, f32),
             pltpu.VMEM((samples, tables, bag_size), i32),
@@ -513,7 +518,8 @@
             pltpu.VMEM((depths, rows) + block, f32),
             pltpu.VMEM((tables, rows_dev, depths * rows * samples), jnp.bfloat16),
             pltpu.VMEM(table.shape, f32),
-            dma((tables,)),
+            pltpu.VMEM((1, samples), f32),
+            dma((tables + 1,)),
             dma((rows - 1,)),
             dma((rows,)),
             dma((half - 1,)),

time: 30.3 us -> 29.7 us (0.980)
  Pallas kernels: 29.4 us -> 28.8 us
    pallas_call x1, Pallas kernels: 26.9 us -> 26.3 us  [shards_small(): pl.pallas_call(step_kernel, out_shape=[jax.ShapeDtypeStruct(table.shape,...]
where the time goes in v4:
time: 29.7 us; the launch traced here: 29.5 us
  Pallas kernels  28.8 us (97%)
  between operations  0.64 us (2%)
    pallas_call x1, Pallas kernels, shards_small(): pl.pallas_call(step_kernel, out_shape=[jax.ShapeDtypeStruct(table.shape,...  26.3 us
    pallas_call x1, Pallas kernels, shards_small(): pl.pallas_call(update_kernel, out_shape=[jax.ShapeDtypeStruct(table.shape...  2.56 us

profile of v4, /device:TPU:1, one launch (start us, length us, event | category | flops | bytes accessed | tf_op | source)
XLA Modules:
  0.0 29.5 jit_solution(17615686706505705853)
XLA Ops:
  0.6 26.3 %shard_map.112 = (f32[4,256,256]{2,1,0:T(8,128)}, f32[1,8]{1,0:T(1,128)}) custom-call(f32[4,256,256]{2,1,0:T(8,128)} %table_in.3, s32[8,4,64]{2,1,0:T(4,128)} %bitcast.3, s32[8,4,64]{2,1,0:T(4,128)} %local_in.1, s32[4,8]{1,0:T(4,128)} %bitcast.4, s32[8,13]{1,0:T(8,128)} %dense_in.1, s32[8]{0:T(128)} %labels_in.1, f32[13,256]{1,0:T(8,128)} %bottom_in.1, f32[10]{0:T(128)} %top_in.1), custom_call_target="tpu_custom_call" | custom-call | tf_op jit(solution)/shard_map/pallas_call | solution.py:494
  26.9 2.6 %shard_map.113 = (f32[4,256,256]{2,1,0:T(8,128)}, f32[4,256]{1,0:T(4,128)}, f32[1,8]{1,0:T(1,128)}) custom-call(f32[4,256,256]{2,1,0:T(8,128)} %get-tuple-element.8.grad_in, f32[4,256,256]{2,1,0:T(8,128)} %table_in.3, f32[4,256]{1,0:T(4,128)} %accum_in.1, f32[1,8]{1,0:T(1,128)} %get-tuple-element.9.logits_in), custom_call_target="tpu_custom_call" | custom-call | tf_op jit(solution)/shard_map/pallas_call | solution.py:546
